TPU v7x, 32 devices: a whole 2x2x4 slice. The times are simulated.
32 devices in a mesh: groups: 2 (over y), col: 4 (over z), row: 2 (over x), sub: 2 (over core).
Axes of the slice: x: 2, y: 2, z: 4, core: 2. Of those that a mesh axis runs over, the one named last changes fastest.
Arguments:
- amps: float32 [1536, 69632], P(('groups', 'row'), ('col', 'sub')), parts along dimension 0, may hold values from -12 to 12
- integrals: float32 [139264, 1024], P(('groups', 'col', 'sub')), parts along dimension 0, may hold values from -0.03125 to 0.03125
- occ_pairs: int32 [768, 2], P('row'), may hold values from 0 to 63, as said below
- slab_pairs: int32 [1024, 2], replicated, may hold values from 0 to 511, as said below
- occ_energy: float32 [128], P('groups'), parts along dimension 0, may hold values from -1.2 to -0.3
- vir_energy: float32 [1024], P('groups'), parts along dimension 0, may hold values from 0.1 to 1.5
Outputs:
- residual: float32 [1536, 1024], P(('groups', 'row'), ('col', 'sub')), parts along dimension 0
- increment: float32 [1536, 1024], P(('groups', 'row'), ('col', 'sub')), parts along dimension 0
There are 2 independent parts, one for each index of `groups`. A program takes and returns all parts, laid end to end along the dimension named above; an argument that names none is the same for every part. Nothing has to cross between parts.
Inputs may be any that keep to these rules, and one draw needn't show every extreme that they name: `occ_pairs`: each row holds two occupied orbitals, the first no larger than the second. `slab_pairs`: each row holds two virtual orbitals, the first no larger than the second.
All inputs are finite; a program needn't handle non-finite values.
Results may differ from a plain program's by a relative error of at most 0.000073.
Values sent between devices are 32-bit elements; how exact they have to be, the bound alone decides.
A program may use at most 128 MiB of HBM per device.

v0:
```python
import jax
import jax.numpy as jnp
from jax import lax
from jax.sharding import PartitionSpec as P


def lookup(table, indices):
    places = jnp.arange(table.shape[0], dtype=jnp.int32)
    return jnp.sum(jnp.where(indices[:, None] == places[None, :], table[None, :], 0.0), axis=1)


def pair_energy(table, pairs):
    return lookup(table, pairs[:, 0]) + lookup(table, pairs[:, 1])


def local(amps, integrals, occ_pairs, slab_pairs, occ_energy, vir_energy):
    width = integrals.shape[1]
    pieces = lax.axis_size(("col", "sub"))
    partial_value = jnp.dot(
        amps, integrals, precision=lax.Precision.HIGHEST, preferred_element_type=jnp.float32
    )
    residual = lax.psum_scatter(partial_value, ("col", "sub"), scatter_dimension=1, tiled=True)
    columns = width // pieces
    first_col = lax.axis_index(("col", "sub")) * columns
    slab_here = lax.dynamic_slice_in_dim(slab_pairs, first_col, columns, 0)
    denominator = (
        pair_energy(occ_energy, occ_pairs)[:, None] - pair_energy(vir_energy, slab_here)[None, :]
    )
    increment = residual / denominator
    return (residual, increment)


def solution(mesh):
    return jax.shard_map(
        local,
        mesh=mesh,
        in_specs=(
            P(("groups", "row"), ("col", "sub")),
            P(("groups", "col", "sub"), None),
            P("row", None),
            P(),
            P("groups"),
            P("groups"),
        ),
        out_specs=(P(("groups", "row"), ("col", "sub")), P(("groups", "row"), ("col", "sub"))),
        check_vma=False,
    )
```

profile of v0, /device:TPU:0, one launch (start us, length us, event | category | flops | bytes accessed | tf_op | source)
XLA Modules:
  0.0 103.1 jit_solution(6038242017384643812)
XLA Ops:
  7.2 0.0 copy-start
  7.2 0.0 copy-start.2
  7.2 0.0 copy-start.1
  7.2 0.0 copy-start.3
  7.2 0.0 reduce-scatter.2.cloned.1.call-start
  7.3 50.1 %fusion = f32[384,1024]{1,0:T(8,128)} fusion(f32[384,8704]{1,0:T(8,128)} %param.6, f32[8704,1024]{1,0:T(8,128)} %param.7), kind=kOutput, calls=%fused_computation.14 | convolution fusion | flops 41070624768 | bytes 50593792 | tf_op jit(solution)/shard_map/dot_general | solution.py:19
  57.4 0.0 reduce-scatter.2.cloned.1.call-update
  57.4 0.0 copy-done
  57.4 0.0 copy-done.2
  57.5 0.2 select_reduce_fusion
  57.7 0.0 copy-done.1
  57.7 0.0 copy-done.3
  57.7 0.1 select_reduce_fusion.2
  57.8 36.7 %reduce-scatter.2.cloned.1.call-done = f32[384,128]{1,0:T(8,128)} async-done(((f32[384,1024]{1,0:T(8,128)}), f32[384,128]{1,0:T(8,128)}) %reduce-scatter.2.cloned.1.call-update) | async-done | bytes 196624 | tf_op jit(solution)/shard_map/reduce_scatter | solution.py:22
  94.5 1.7 %subtract_divide_fusion = f32[384,128]{1,0:T(8,128)} fusion(f32[384,128]{1,0:T(8,128)} %reduce-scatter.2.cloned.1.call-done, f32[128]{0:T(128)S(1)} %add.25, f32[384]{0:T(512)S(1)} %add.22), kind=kLoop, calls=%fused_computation.4 | loop fusion | flops 98304 | bytes 395264 | tf_op jit(solution)/shard_map/div | solution.py:29
  (5 shorter events, 0.0 us)
Async XLA Ops:
  7.2 50.2 %copy-start = (s32[1024,2]{0,1:T(2,128)S(1)}, s32[1024,2]{0,1:T(2,128)}, u32[]{:S(2)}) copy-start(s32[1024,2]{0,1:T(2,128)} %param.9) | copy-start | bytes 24580
  7.2 50.3 %copy-start.2 = (f32[512]{0:T(512)S(1)}, f32[512]{0:T(512)}, u32[]{:S(2)}) copy-start(f32[512]{0:T(512)} %param.11) | copy-start | bytes 6148
  7.2 50.5 %copy-start.1 = (s32[384,2]{0,1:T(2,128)S(1)}, s32[384,2]{0,1:T(2,128)}, u32[]{:S(2)}) copy-start(s32[384,2]{0,1:T(2,128)} %param.8) | copy-start | bytes 9220
  7.2 50.5 %copy-start.3 = (f32[64]{0:T(128)S(1)}, f32[64]{0:T(128)}, u32[]{:S(2)}) copy-start(f32[64]{0:T(128)} %param.10) | copy-start | bytes 772
  7.2 87.3 %reduce-scatter.2.cloned.1.call-start = ((), (), s32[]{:S(2)}) async-start(), calls=%async_computation.1 | async-start | bytes 1769472 | tf_op jit(solution)/shard_map/reduce_scatter | solution.py:22
Sparse Core Ops, SparseCore 0:
  57.5 36.9 reduce-scatter.1
where the time goes:
time: 103 us
  matrix products  50.1 us (49%)
  waiting for transfers between devices  36.7 us (36%)
  between operations  14.1 us (14%)
  other arithmetic  2.04 us (2%)
    dot_general x1, matrix products, local(): jnp.dot(amps, integrals, precision=lax.Precision.HIGHEST, preferred_eleme...  50.1 us
    reduce_scatter x1, waiting for transfers between devices, local(): lax.psum_scatter(partial_value, ('col', 'sub'), scatter_dimension=1, tile...  36.7 us
  transfers between devices with their start and end apart: 1, of which 1 were waited for; matrix products, arithmetic and copies ran while one was open for 0% of the time, Pallas kernels for 0%

commit v1 on v0

--- a/solution.py
+++ b/solution.py
@@ -1,7 +1,15 @@
+import functools
+
 import jax
 import jax.numpy as jnp
 from jax import lax
+from jax.experimental import pallas as pl
+from jax.experimental.pallas import tpu as pltpu
 from jax.sharding import PartitionSpec as P
+
+LANES = 128
+CHUNKS = 17
+MESH = pl.DeviceIdType.MESH
 
 
 def lookup(table, indices):
@@ -13,11 +21,11 @@
     return lookup(table, pairs[:, 0]) + lookup(table, pairs[:, 1])
 
 
-def local(amps, integrals, occ_pairs, slab_pairs, occ_energy, vir_energy):
+def plain(amps, integrals, occ_pairs, slab_pairs, occ_energy, vir_energy):
     width = integrals.shape[1]
     pieces = lax.axis_size(("col", "sub"))
     partial_value = jnp.dot(
-        amps, integrals, precision=lax.Precision.HIGHEST, preferred_element_type=jnp.float32
+        amps, integrals, precision=lax.Precision.HIGH, preferred_element_type=jnp.float32
     )
     residual = lax.psum_scatter(partial_value, ("col", "sub"), scatter_dimension=1, tiled=True)
     columns = width // pieces
@@ -28,6 +36,253 @@
     )
     increment = residual / denominator
     return (residual, increment)
+
+
+def column_of(row):
+    n = row.shape[1]
+    here = lax.broadcasted_iota(jnp.int32, (n, n), 0) == lax.broadcasted_iota(jnp.int32, (n, n), 1)
+    return jnp.sum(jnp.where(here, jnp.broadcast_to(row, (n, n)), 0.0), axis=1, keepdims=True)
+
+
+def table_row(table, indices):
+    shape = (table.shape[0], indices.shape[1])
+    places = lax.broadcasted_iota(jnp.int32, shape, 0)
+    picked = jnp.where(places == jnp.broadcast_to(indices, shape), jnp.broadcast_to(table, shape), 0.0)
+    return jnp.sum(picked, axis=0, keepdims=True)
+
+
+def split(values):
+    high = values.astype(jnp.bfloat16)
+    return high, (values - high.astype(jnp.float32)).astype(jnp.bfloat16)
+
+
+def dot(a, b):
+    return jnp.dot(a, b, preferred_element_type=jnp.float32)
+
+
+def ladder(
+    cols_n, amps, integrals, occ_t, slab_t, occ_e, vir_e, residual, increment,
+    wide, halves, blocks, acc, denom, outbox, inbox, mine, arrived,
+    wide_sem, block_sem, swap_send, swap_recv, hop_send, hop_recv,
+):
+    rows = amps.shape[0]
+    depth = wide.shape[2]
+    last = cols_n - 1
+    col, sub = lax.axis_index("col"), lax.axis_index("sub")
+
+    def order(j):
+        return (last * (1 - col // 2), (3 * col + 2) % 5, 1 + col % 2, col)[j]
+
+    def way(j):
+        return (col // 2, col % 2, col // 2)[j]
+
+    def load_wide(k):
+        return pltpu.make_async_copy(
+            amps.at[:, pl.ds(pl.multiple_of(k * depth, depth), depth)], wide.at[k], wide_sem.at[k]
+        )
+
+    def load_block(j, k):
+        return pltpu.make_async_copy(
+            integrals.at[
+                pl.ds(pl.multiple_of(k * depth, depth), depth),
+                pl.ds(pl.multiple_of(order(j) * 2 * LANES, 2 * LANES), 2 * LANES),
+            ],
+            blocks.at[j % 2, k],
+            block_sem.at[j % 2, k],
+        )
+
+    def swap(j):
+        return pltpu.make_async_remote_copy(
+            src_ref=outbox.at[j], dst_ref=inbox.at[j],
+            send_sem=swap_send.at[j], recv_sem=swap_recv.at[j],
+            device_id={"sub": 1 - sub}, device_id_type=MESH,
+        )
+
+    def hop(j):
+        return pltpu.make_async_remote_copy(
+            src_ref=mine.at[j], dst_ref=arrived.at[way(j), order(j)],
+            send_sem=hop_send.at[j], recv_sem=hop_recv.at[way(j), order(j)],
+            device_id={"col": col + 1 - 2 * way(j)}, device_id_type=MESH,
+        )
+
+    def arrival(d, target):
+        return pltpu.make_async_remote_copy(
+            src_ref=mine.at[0], dst_ref=arrived.at[d, target],
+            send_sem=hop_send.at[0], recv_sem=hop_recv.at[d, target],
+            device_id={"col": col}, device_id_type=MESH,
+        )
+
+    @pl.loop(0, CHUNKS)
+    def _(k):
+        load_wide(k).start()
+        load_block(0, k).start()
+
+    @pl.loop(0, CHUNKS)
+    def _(k):
+        load_block(1, k).start()
+
+    barrier = pltpu.get_barrier_semaphore()
+    inner = (col > 0) & (col < last)
+    pl.semaphore_signal(barrier, inc=1, device_id={"sub": 1 - sub}, device_id_type=MESH)
+
+    @pl.when(col > 0)
+    def _():
+        pl.semaphore_signal(barrier, inc=1, device_id={"col": col - 1}, device_id_type=MESH)
+
+    @pl.when(col < last)
+    def _():
+        pl.semaphore_signal(barrier, inc=1, device_id={"col": col + 1}, device_id_type=MESH)
+
+    occ_table = column_of(occ_e[...])
+    vir_table = jnp.concatenate(
+        [column_of(vir_e[:, at : at + LANES]) for at in range(0, vir_e.shape[1], LANES)], axis=0
+    )
+    own = pl.multiple_of((2 * col + sub) * LANES, LANES)
+    slab = slab_t[:, pl.ds(own, LANES)]
+    vir_row = table_row(vir_table, slab[0:1, :]) + table_row(vir_table, slab[1:2, :])
+    for at in range(0, rows, LANES):
+        pairs = occ_t[:, at : at + LANES]
+        occ_row = table_row(occ_table, pairs[0:1, :]) + table_row(occ_table, pairs[1:2, :])
+        denom[at : at + LANES, :] = column_of(occ_row) - vir_row
+
+    @pl.when(inner)
+    def _():
+        pl.semaphore_wait(barrier, 3)
+
+    @pl.when(jnp.logical_not(inner))
+    def _():
+        pl.semaphore_wait(barrier, 2)
+
+    def multiply(j, k):
+        load_block(j, k).wait()
+        if j == 0:
+            load_wide(k).wait()
+            a_high, a_low = split(wide[k])
+            halves[k, :rows, :] = a_high
+            halves[k, rows:, :] = a_low
+        b_high, b_low = split(blocks[j % 2, k])
+        both = dot(halves[k], b_high)
+        term = both[:rows] + both[rows:] + dot(halves[k, :rows, :], b_low)
+        acc[...] += term
+        if j + 2 < cols_n:
+            load_block(j + 2, k).start()
+
+    def gather_swap(j):
+        swap(j).wait_recv()
+        mine[j] += inbox[j]
+
+    def forward(j):
+        arrival(way(j), order(j)).wait_recv()
+        mine[j] += arrived[way(j), order(j)]
+        hop(j).start()
+
+    early, mid = 6, 10
+    for j in range(cols_n):
+        acc[...] = jnp.zeros_like(acc)
+
+        @pl.loop(0, early)
+        def _(k):
+            multiply(j, k)
+
+        if j >= 1:
+            gather_swap(j - 1)
+
+            @pl.when(jnp.logical_not(inner))
+            def _():
+                hop(j - 1).start()
+
+        @pl.loop(early, mid)
+        def _(k):
+            multiply(j, k)
+
+        if j >= 2:
+
+            @pl.when(inner)
+            def _():
+                forward(j - 2)
+
+        @pl.loop(mid, CHUNKS)
+        def _(k):
+            multiply(j, k)
+
+        left, right = acc[:, :LANES], acc[:, LANES:]
+        first = sub == 0
+        mine[j] = jnp.where(first, left, right)
+        outbox[j] = jnp.where(first, right, left)
+        swap(j).start()
+
+    @pl.when(inner)
+    def _():
+        forward(cols_n - 2)
+
+    gather_swap(last)
+
+    @pl.when(col > 0)
+    def _():
+        arrival(0, col).wait_recv()
+        mine[last] += arrived[0, col]
+
+    @pl.when(col < last)
+    def _():
+        arrival(1, col).wait_recv()
+        mine[last] += arrived[1, col]
+
+    total = mine[last]
+    residual[...] = total
+    increment[...] = total / denom[...]
+    for j in range(cols_n):
+        swap(j).wait_send()
+        if j < last:
+            hop(j).wait_send()
+
+
+def local(amps, integrals, occ_pairs, slab_pairs, occ_energy, vir_energy):
+    rows, depth = amps.shape
+    width = integrals.shape[1]
+    cols_n, subs = lax.axis_size("col"), lax.axis_size("sub")
+    fits = (
+        cols_n == 4 and subs == 2 and width == cols_n * subs * LANES
+        and depth % (CHUNKS * LANES) == 0 and rows % LANES == 0
+        and vir_energy.shape[0] % LANES == 0
+    )
+    if not fits:
+        return plain(amps, integrals, occ_pairs, slab_pairs, occ_energy, vir_energy)
+    piece = depth // CHUNKS
+    f32, bf16 = jnp.float32, jnp.bfloat16
+    dma = pltpu.SemaphoreType.DMA
+    vmem = pl.BlockSpec(memory_space=pltpu.VMEM)
+    hbm = pl.BlockSpec(memory_space=pl.ANY)
+    return pl.pallas_call(
+        functools.partial(ladder, cols_n),
+        out_shape=[jax.ShapeDtypeStruct((rows, LANES), f32)] * 2,
+        in_specs=[hbm, hbm, vmem, vmem, vmem, vmem],
+        out_specs=[vmem, vmem],
+        scratch_shapes=[
+            pltpu.VMEM((CHUNKS, rows, piece), f32),
+            pltpu.VMEM((CHUNKS, 2 * rows, piece), bf16),
+            pltpu.VMEM((2, CHUNKS, piece, 2 * LANES), f32),
+            pltpu.VMEM((rows, 2 * LANES), f32),
+            pltpu.VMEM((rows, LANES), f32),
+            pltpu.VMEM((cols_n, rows, LANES), f32),
+            pltpu.VMEM((cols_n, rows, LANES), f32),
+            pltpu.VMEM((cols_n, rows, LANES), f32),
+            pltpu.VMEM((2, cols_n, rows, LANES), f32),
+            dma((CHUNKS,)),
+            dma((2, CHUNKS)),
+            dma((cols_n,)),
+            dma((cols_n,)),
+            dma((cols_n,)),
+            dma((2, cols_n)),
+        ],
+        compiler_params=pltpu.CompilerParams(
+            collective_id=0, has_side_effects=True, vmem_limit_bytes=60 * 1024 * 1024
+        ),
+        cost_estimate=pl.CostEstimate(
+            flops=6 * rows * depth * width,
+            bytes_accessed=4 * depth * (rows + width),
+            transcendentals=0,
+        ),
+    )(amps, integrals, occ_pairs.T, slab_pairs.T, occ_energy[None, :], vir_energy[None, :])
 
 
 def solution(mesh):

time: 103 us -> 47.7 us (0.46)
  the two profiles are of different devices: /device:TPU:0 before, /device:TPU:12 now
where the time goes in v1:
time: 47.7 us; the launch traced here: 47.5 us
  Pallas kernels  43.6 us (91%)
  local copies, waits for them, and re-layouts  3.23 us (7%)
  between operations  0.64 us (1%)
    pallas_call x1, Pallas kernels, local(): pl.pallas_call(functools.partial(ladder, cols_n), out_shape=[jax.ShapeDty...  43.6 us
    unnamed x2, local copies, waits for them, and re-layouts  3.23 us

profile of v1, /device:TPU:12, one launch (start us, length us, event | category | flops | bytes accessed | tf_op | source)
XLA Modules:
  0.0 47.5 jit_solution(9108352454629973607)
XLA Ops:
  0.6 43.6 %shard_map.77 = (f32[384,128]{1,0:T(8,128)}, f32[384,128]{1,0:T(8,128)}) custom-call(f32[384,8704]{1,0:T(8,128)} %amps.1, f32[8704,1024]{1,0:T(8,128)} %integrals.1, s32[2,384]{1,0:T(2,128)} %bitcast.5, s32[2,1024]{1,0:T(2,128)} %bitcast.4, f32[1,64]{1,0:T(1,128)} %bitcast.7, f32[1,512]{1,0:T(1,128)} %bitcast.6), custom_call_target="tpu_custom_call" | custom-call | flops 20535312384 | bytes 49020928 | tf_op jit(solution)/shard_map/pallas_call | solution.py:255
  44.2 1.6 %copy.10 = f32[384,128]{1,0:T(8,128)} copy(f32[384,128]{1,0:T(8,128)} %get-tuple-element.4) | data formatting | bytes 393216
  45.8 1.6 %copy.11 = f32[384,128]{1,0:T(8,128)} copy(f32[384,128]{1,0:T(8,128)} %get-tuple-element.5) | data formatting | bytes 393216

commit v2 on v1

--- a/solution.py
+++ b/solution.py
@@ -8,7 +8,8 @@
 from jax.sharding import PartitionSpec as P
 
 LANES = 128
-CHUNKS = 17
+CHUNKS = 4
+FORWARD = ((9, 0), (13, 1), (14, 2))
 MESH = pl.DeviceIdType.MESH
 
 
@@ -61,8 +62,8 @@
 
 
 def ladder(
-    cols_n, amps, integrals, occ_t, slab_t, occ_e, vir_e, residual, increment,
-    wide, halves, blocks, acc, denom, outbox, inbox, mine, arrived,
+    cols_n, amps, integrals, occ_t, slab_t, occ_e, vir_e, near, far, denom,
+    wide, left_hand, blocks, acc, outbox, inbox, mine, arrived,
     wide_sem, block_sem, swap_send, swap_recv, hop_send, hop_recv,
 ):
     rows = amps.shape[0]
@@ -71,24 +72,31 @@
     col, sub = lax.axis_index("col"), lax.axis_index("sub")
 
     def order(j):
-        return (last * (1 - col // 2), (3 * col + 2) % 5, 1 + col % 2, col)[j]
+        return (
+            (1 - (j + 2) // 3) * last * (1 - col // 2)
+            + (j % 2) * (1 - j // 3) * ((3 * col + 2) % 5)
+            + (1 - j % 2) * (j // 2) * (1 + col % 2)
+            + (j // 3) * col
+        )
 
     def way(j):
-        return (col // 2, col % 2, col // 2)[j]
+        return (1 - j % 2) * (col // 2) + (j % 2) * (col % 2)
 
     def load_wide(k):
         return pltpu.make_async_copy(
             amps.at[:, pl.ds(pl.multiple_of(k * depth, depth), depth)], wide.at[k], wide_sem.at[k]
         )
 
-    def load_block(j, k):
+    def load_block(step):
+        j, k = step // CHUNKS, step % CHUNKS
+        slot = step % (2 * CHUNKS)
         return pltpu.make_async_copy(
             integrals.at[
                 pl.ds(pl.multiple_of(k * depth, depth), depth),
                 pl.ds(pl.multiple_of(order(j) * 2 * LANES, 2 * LANES), 2 * LANES),
             ],
-            blocks.at[j % 2, k],
-            block_sem.at[j % 2, k],
+            blocks.at[slot],
+            block_sem.at[slot],
         )
 
     def swap(j):
@@ -115,11 +123,11 @@
     @pl.loop(0, CHUNKS)
     def _(k):
         load_wide(k).start()
-        load_block(0, k).start()
-
-    @pl.loop(0, CHUNKS)
+        load_block(k).start()
+
+    @pl.loop(CHUNKS, 2 * CHUNKS)
     def _(k):
-        load_block(1, k).start()
+        load_block(k).start()
 
     barrier = pltpu.get_barrier_semaphore()
     inner = (col > 0) & (col < last)
@@ -153,20 +161,6 @@
     def _():
         pl.semaphore_wait(barrier, 2)
 
-    def multiply(j, k):
-        load_block(j, k).wait()
-        if j == 0:
-            load_wide(k).wait()
-            a_high, a_low = split(wide[k])
-            halves[k, :rows, :] = a_high
-            halves[k, rows:, :] = a_low
-        b_high, b_low = split(blocks[j % 2, k])
-        both = dot(halves[k], b_high)
-        term = both[:rows] + both[rows:] + dot(halves[k, :rows, :], b_low)
-        acc[...] += term
-        if j + 2 < cols_n:
-            load_block(j + 2, k).start()
-
     def gather_swap(j):
         swap(j).wait_recv()
         mine[j] += inbox[j]
@@ -176,44 +170,58 @@
         mine[j] += arrived[way(j), order(j)]
         hop(j).start()
 
-    early, mid = 6, 10
-    for j in range(cols_n):
-        acc[...] = jnp.zeros_like(acc)
-
-        @pl.loop(0, early)
-        def _(k):
-            multiply(j, k)
-
-        if j >= 1:
+    steps = cols_n * CHUNKS
+
+    @pl.loop(0, steps)
+    def _(step):
+        j, k = step // CHUNKS, step % CHUNKS
+        slot = step % (2 * CHUNKS)
+
+        @pl.when(step < CHUNKS)
+        def _():
+            load_wide(k).wait()
+            high, low = split(wide[k])
+            left_hand[k, :, :depth] = high
+            left_hand[k, :, depth:] = low
+
+        load_block(step).wait()
+        b_high, b_low = split(blocks[slot])
+        value = dot(left_hand[k], jnp.concatenate([b_high, b_high], axis=0))
+        value += dot(left_hand[k, :, :depth], b_low)
+
+        @pl.when(k == 0)
+        def _():
+            acc[...] = value
+
+        @pl.when(k > 0)
+        def _():
+            acc[...] += value
+
+        @pl.when(step + 2 * CHUNKS < steps)
+        def _():
+            load_block(step + 2 * CHUNKS).start()
+
+        @pl.when((k == 0) & (j >= 1))
+        def _():
             gather_swap(j - 1)
 
             @pl.when(jnp.logical_not(inner))
             def _():
                 hop(j - 1).start()
 
-        @pl.loop(early, mid)
-        def _(k):
-            multiply(j, k)
-
-        if j >= 2:
-
-            @pl.when(inner)
+        for when, passed in FORWARD:
+
+            @pl.when((step == when) & inner)
             def _():
-                forward(j - 2)
-
-        @pl.loop(mid, CHUNKS)
-        def _(k):
-            multiply(j, k)
-
-        left, right = acc[:, :LANES], acc[:, LANES:]
-        first = sub == 0
-        mine[j] = jnp.where(first, left, right)
-        outbox[j] = jnp.where(first, right, left)
-        swap(j).start()
-
-    @pl.when(inner)
-    def _():
-        forward(cols_n - 2)
+                forward(passed)
+
+        @pl.when(k == CHUNKS - 1)
+        def _():
+            left, right = acc[:, :LANES], acc[:, LANES:]
+            first = sub == 0
+            mine[j] = jnp.where(first, left, right)
+            outbox[j] = jnp.where(first, right, left)
+            swap(j).start()
 
     gather_swap(last)
 
@@ -222,14 +230,17 @@
         arrival(0, col).wait_recv()
         mine[last] += arrived[0, col]
 
+    near[...] = mine[last]
+
     @pl.when(col < last)
     def _():
         arrival(1, col).wait_recv()
-        mine[last] += arrived[1, col]
-
-    total = mine[last]
-    residual[...] = total
-    increment[...] = total / denom[...]
+        far[...] = arrived[1, col]
+
+    @pl.when(col == last)
+    def _():
+        far[...] = jnp.zeros_like(far)
+
     for j in range(cols_n):
         swap(j).wait_send()
         if j < last:
@@ -252,30 +263,29 @@
     dma = pltpu.SemaphoreType.DMA
     vmem = pl.BlockSpec(memory_space=pltpu.VMEM)
     hbm = pl.BlockSpec(memory_space=pl.ANY)
-    return pl.pallas_call(
+    near, far, denom = pl.pallas_call(
         functools.partial(ladder, cols_n),
-        out_shape=[jax.ShapeDtypeStruct((rows, LANES), f32)] * 2,
+        out_shape=[jax.ShapeDtypeStruct((rows, LANES), f32)] * 3,
         in_specs=[hbm, hbm, vmem, vmem, vmem, vmem],
-        out_specs=[vmem, vmem],
+        out_specs=[vmem, vmem, vmem],
         scratch_shapes=[
             pltpu.VMEM((CHUNKS, rows, piece), f32),
-            pltpu.VMEM((CHUNKS, 2 * rows, piece), bf16),
-            pltpu.VMEM((2, CHUNKS, piece, 2 * LANES), f32),
+            pltpu.VMEM((CHUNKS, rows, 2 * piece), bf16),
+            pltpu.VMEM((2 * CHUNKS, piece, 2 * LANES), f32),
             pltpu.VMEM((rows, 2 * LANES), f32),
-            pltpu.VMEM((rows, LANES), f32),
             pltpu.VMEM((cols_n, rows, LANES), f32),
             pltpu.VMEM((cols_n, rows, LANES), f32),
             pltpu.VMEM((cols_n, rows, LANES), f32),
             pltpu.VMEM((2, cols_n, rows, LANES), f32),
             dma((CHUNKS,)),
-            dma((2, CHUNKS)),
+            dma((2 * CHUNKS,)),
             dma((cols_n,)),
             dma((cols_n,)),
             dma((cols_n,)),
             dma((2, cols_n)),
         ],
         compiler_params=pltpu.CompilerParams(
-            collective_id=0, has_side_effects=True, vmem_limit_bytes=60 * 1024 * 1024
+            collective_id=0, has_side_effects=True, vmem_limit_bytes=62 * 1024 * 1024
         ),
         cost_estimate=pl.CostEstimate(
             flops=6 * rows * depth * width,
@@ -283,6 +293,8 @@
             transcendentals=0,
         ),
     )(amps, integrals, occ_pairs.T, slab_pairs.T, occ_energy[None, :], vir_energy[None, :])
+    residual = near + far
+    return residual, residual / denom
 
 
 def solution(mesh):

time: 47.7 us -> 39.6 us (0.83)
  Pallas kernels: 43.6 us -> 36.8 us
  local copies, waits for them, and re-layouts: 3.23 us -> 0 us
  other arithmetic: 0 us -> 1.89 us
    pallas_call x1, Pallas kernels: 43.6 us -> 36.8 us  [local(): pl.pallas_call(functools.partial(ladder, cols_n), out_shape=[jax.ShapeDty...]
    unnamed x2 -> x0, local copies, waits for them, and re-layouts: 3.23 us -> none
    div x0 -> x1, other arithmetic: none -> 1.89 us  [local(): return (residual, residual / denom)]
where the time goes in v2:
time: 39.6 us; the launch traced here: 39.4 us
  Pallas kernels  36.8 us (93%)
  other arithmetic  1.89 us (5%)
  between operations  0.64 us (2%)
    pallas_call x1, Pallas kernels, local(): pl.pallas_call(functools.partial(ladder, cols_n), out_shape=[jax.ShapeDty...  36.8 us
    div x1, other arithmetic, local(): return (residual, residual / denom)  1.89 us

profile of v2, /device:TPU:12, one launch (start us, length us, event | category | flops | bytes accessed | tf_op | source)
XLA Modules:
  0.0 39.4 jit_solution(16726150652389008435)
XLA Ops:
  0.6 36.8 %shard_map.77 = (f32[384,128]{1,0:T(8,128)}, f32[384,128]{1,0:T(8,128)}, f32[384,128]{1,0:T(8,128)}) custom-call(f32[384,8704]{1,0:T(8,128)} %amps.1, f32[8704,1024]{1,0:T(8,128)} %integrals.1, s32[2,384]{1,0:T(2,128)} %bitcast.5, s32[2,1024]{1,0:T(2,128)} %bitcast.4, f32[1,64]{1,0:T(1,128)} %bitcast.7, f32[1,512]{1,0:T(1,128)} %bitcast.6), custom_call_target="tpu_custom_call" | custom-call | flops 20535312384 | bytes 49020928 | tf_op jit(solution)/shard_map/pallas_call | solution.py:266
  37.5 1.9 %fusion = (f32[384,128]{1,0:T(8,128)}, f32[384,128]{1,0:T(8,128)}) fusion(f32[384,128]{1,0:T(8,128)} %get-tuple-element.7, f32[384,128]{1,0:T(8,128)} %get-tuple-element.5, f32[384,128]{1,0:T(8,128)} %get-tuple-element.6), kind=kLoop, calls=%fused_computation | loop fusion | flops 98304 | bytes 983040 | tf_op jit(solution)/shard_map/div | solution.py:297

commit v3 on v2

--- a/solution.py
+++ b/solution.py
@@ -170,6 +170,7 @@
         mine[j] += arrived[way(j), order(j)]
         hop(j).start()
 
+    acc[...] = jnp.zeros_like(acc)
     steps = cols_n * CHUNKS
 
     @pl.loop(0, steps)
@@ -189,13 +190,7 @@
         value = dot(left_hand[k], jnp.concatenate([b_high, b_high], axis=0))
         value += dot(left_hand[k, :, :depth], b_low)
 
-        @pl.when(k == 0)
-        def _():
-            acc[...] = value
-
-        @pl.when(k > 0)
-        def _():
-            acc[...] += value
+        acc[...] = jnp.where(k == 0, value, acc[...] + value)
 
         @pl.when(step + 2 * CHUNKS < steps)
         def _():

time: 39.6 us -> 38.8 us (0.980)
  Pallas kernels: 36.8 us -> 36 us
    pallas_call x1, Pallas kernels: 36.8 us -> 36 us  [local(): pl.pallas_call(functools.partial(ladder, cols_n), out_shape=[jax.ShapeDty...]
where the time goes in v3:
time: 38.8 us; the launch traced here: 38.5 us
  Pallas kernels  36 us (93%)
  other arithmetic  1.89 us (5%)
  between operations  0.64 us (2%)
    pallas_call x1, Pallas kernels, local(): pl.pallas_call(functools.partial(ladder, cols_n), out_shape=[jax.ShapeDty...  36 us
    div x1, other arithmetic, local(): return (residual, residual / denom)  1.89 us

profile of v3, /device:TPU:12, one launch (start us, length us, event | category | flops | bytes accessed | tf_op | source)
XLA Modules:
  0.0 38.5 jit_solution(9468332990013127374)
XLA Ops:
  0.6 36.0 %shard_map.77 = (f32[384,128]{1,0:T(8,128)}, f32[384,128]{1,0:T(8,128)}, f32[384,128]{1,0:T(8,128)}) custom-call(f32[384,8704]{1,0:T(8,128)} %amps.1, f32[8704,1024]{1,0:T(8,128)} %integrals.1, s32[2,384]{1,0:T(2,128)} %bitcast.5, s32[2,1024]{1,0:T(2,128)} %bitcast.4, f32[1,64]{1,0:T(1,128)} %bitcast.7, f32[1,512]{1,0:T(1,128)} %bitcast.6), custom_call_target="tpu_custom_call" | custom-call | flops 20535312384 | bytes 49020928 | tf_op jit(solution)/shard_map/pallas_call | solution.py:261
  36.7 1.9 %fusion = (f32[384,128]{1,0:T(8,128)}, f32[384,128]{1,0:T(8,128)}) fusion(f32[384,128]{1,0:T(8,128)} %get-tuple-element.7, f32[384,128]{1,0:T(8,128)} %get-tuple-element.5, f32[384,128]{1,0:T(8,128)} %get-tuple-element.6), kind=kLoop, calls=%fused_computation | loop fusion | flops 98304 | bytes 983040 | tf_op jit(solution)/shard_map/div | solution.py:292
